TPU v7x, 32 devices: a whole 2x2x4 slice. The times are simulated.
32 devices in a mesh: xy: 8 (over z, y), gz: 4 (over x, core).
Axes of the slice: x: 2, y: 2, z: 4, core: 2. Of those that a mesh axis runs over, the one named last changes fastest.
Arguments:
- base_field: bfloat16 [132, 32, 32, 256], P(None, 'gz', 'xy'), may hold values from 0 to 2
- increments: bfloat16 [132, 262144], P(None, ('xy', 'gz')), may hold values from -6 to 6
- dest_tile: int32 [262144, 1], P(('xy', 'gz')), may hold values from 0 to 7; in each aligned block of 8192 rows (0 to 8191, 8192 to 16383, ...) at most 2048 rows name the same one
- dest_cell: int32 [262144], P(('xy', 'gz')), may hold values from 0 to 8191
- courant_x: bfloat16 [32, 32, 256], P('gz', 'xy'), may hold values from -0.23925781 to 0.23925781
- courant_y: bfloat16 [32, 32, 256], P('gz', 'xy'), may hold values from -0.23925781 to 0.23925781
- fall_courant: float32 [132, 32], replicated, may hold values from 0.001 to 280
Outputs:
- settled: bfloat16 [132, 32, 32, 256], P(None, 'gz', 'xy')
Inputs may be any that keep to these rules, and one draw needn't show every extreme that they name: `dest_tile`: among the rows of one device, at most 2048 name the same tile; in every draw some device has exactly 2048 rows naming one tile.
All inputs are finite; a program needn't handle non-finite values.
Results may differ from a plain program's by a relative error of at most 0.0043.
Values may be sent and summed in bfloat16 or wider, within the bound.
A program may use at most 128 MiB of HBM per device.

v0:
```python
import jax
import jax.numpy as jnp
from jax import lax
from jax.sharding import PartitionSpec as P


def shifted(value, axis, steps):
    count = lax.axis_size(axis)
    first, last = (max(0, -steps), min(count, count - steps))
    return lax.ppermute(value, axis, [(source, source + steps) for source in range(first, last)])


def settle(values, fall_rates, inflow):
    level_count = values.shape[1]

    def descend(counter, state_pair):
        output, current_inflow = state_pair
        level_index = level_count - 1 - counter
        layer = lax.dynamic_slice_in_dim(values, level_index, 1, 1)[:, 0]
        courant = lax.dynamic_slice_in_dim(fall_rates, level_index, 1, 1)[:, :, None]
        value = (layer + current_inflow) / (1.0 + courant)
        output = lax.dynamic_update_slice_in_dim(output, value[:, None], level_index, 1)
        return (output, courant * value)

    return lax.fori_loop(0, level_count, descend, (jnp.zeros_like(values), inflow))


def per_device(base_field, increments, dest_tile, dest_cell, courant_x, courant_y, fall_courant):
    comps, slab_levels, xcells, ycells = base_field.shape
    row_count = increments.shape[1]
    peer_count = lax.axis_size("xy")
    capacity = 2 * row_count // peer_count
    targets = dest_tile[:, 0]
    one_hot = (targets[:, None] == jnp.arange(peer_count, dtype=jnp.int32)[None, :]).astype(
        jnp.int32
    )
    position = jnp.sum(jnp.cumsum(one_hot, axis=0) * one_hot, axis=1) - 1
    slot_index = targets * capacity + position
    packed = (
        jnp.zeros((comps, peer_count * capacity), jnp.bfloat16).at[:, slot_index].set(increments)
    )
    cell_ids = jnp.zeros((1, peer_count * capacity), jnp.int32).at[0, slot_index].set(dest_cell)
    arrived, arrived_cells = (
        lax.all_to_all(packed, "xy", split_axis=1, concat_axis=1, tiled=True),
        lax.all_to_all(cell_ids, "xy", split_axis=1, concat_axis=1, tiled=True),
    )
    summed = (
        jnp.zeros((comps, slab_levels * xcells * ycells), jnp.float32)
        .at[:, arrived_cells[0]]
        .add(arrived.astype(jnp.float32))
    )
    updated = (
        base_field.astype(jnp.float32) + summed.reshape(comps, slab_levels, xcells, ycells)
    ).astype(jnp.bfloat16)
    updated = lax.optimization_barrier(updated)
    current = updated.astype(jnp.float32)
    face_x = courant_x.astype(jnp.float32)
    face_y = courant_y.astype(jnp.float32)
    column_iota = lax.broadcasted_iota(jnp.int32, (slab_levels, xcells, ycells), 1)
    wall_mask = jnp.logical_and(lax.axis_index("xy") == 0, column_iota == 0)
    left_cells = shifted(updated[:, :, xcells - 1 :], "xy", 1)
    from_left = jnp.concatenate([left_cells, updated[:, :, : xcells - 1]], axis=2).astype(
        jnp.float32
    )
    flux_west = jnp.maximum(face_x, 0.0) * from_left + jnp.minimum(face_x, 0.0) * current
    flux_west = jnp.where(wall_mask, 0.0, flux_west)
    edge_flux = shifted(flux_west[:, :, :1].astype(jnp.bfloat16), "xy", -1).astype(jnp.float32)
    flux_east = jnp.concatenate([flux_west[:, :, 1:], edge_flux], axis=2)
    from_below = jnp.pad(current, ((0, 0), (0, 0), (0, 0), (1, 0)))[:, :, :, :-1]
    flux_south = jnp.maximum(face_y, 0.0) * from_below + jnp.minimum(face_y, 0.0) * current
    row_iota = lax.broadcasted_iota(jnp.int32, (slab_levels, xcells, ycells), 2)
    flux_south = jnp.where(row_iota == 0, 0.0, flux_south)
    flux_north = jnp.pad(flux_south[:, :, :, 1:], ((0, 0), (0, 0), (0, 0), (0, 1)))
    advected = (current - (flux_east - flux_west) - (flux_north - flux_south)).astype(jnp.bfloat16)
    column = lax.all_to_all(advected, "gz", split_axis=2, concat_axis=1, tiled=True)
    start = jnp.zeros((comps, column.shape[2], ycells), jnp.float32)
    output, outflow = settle(column.astype(jnp.float32), fall_courant, start)
    result = lax.all_to_all(
        output.astype(jnp.bfloat16), "gz", split_axis=1, concat_axis=2, tiled=True
    )
    return result


def solution(mesh):
    in_specs = (
        P(None, "gz", "xy", None),
        P(None, ("xy", "gz")),
        P(("xy", "gz"), None),
        P(("xy", "gz")),
        P("gz", "xy", None),
        P("gz", "xy", None),
        P(),
    )
    out_specs = P(None, "gz", "xy", None)
    return jax.shard_map(
        per_device, mesh=mesh, in_specs=in_specs, out_specs=out_specs, check_vma=False
    )
```

profile of v0, /device:TPU:24, one launch (start us, length us, event | category | flops | bytes accessed | tf_op | source)
XLA Modules:
  0.0 551.6 jit_solution(12426924624984214190)
XLA Ops:
  0.8 2.4 reduce-window.6
  7.4 31.2 %scatter_custom_fusion.2 = s32[16384]{0:T(1024)} fusion(s32[8192]{0:T(1024)S(1)} %broadcast_select_fusion.1, s32[8192]{0:T(1024)} %param.12, s32[]{:T(128)} %constant.79.clone.1), kind=kCustom, calls=%fused_computation.43 | custom fusion | bytes 66048
  38.6 6.1 %all-to-all-start = ((s32[1,8,2048]{2,0,1:T(1,128)}), s32[1,8,2048]{2,0,1:T(1,128)S(1)}, u32[]{:S(2)}, u32[]{:S(2)}) async-start(s32[1,8,2048]{2,0,1:T(1,128)} %bitcast.4), calls=%async_computation | async-start | bytes 131072 | tf_op jit(solution)/shard_map/all_to_all | solution.py:45
  44.7 5.5 %copy.50 = bf16[8192,132]{1,0:T(8,128)(2,1)} copy(bf16[8192,132]{0,1:T(8,128)(2,1)} %bitcast.62) | data formatting | bytes 4325376 | tf_op args[1]
  50.2 40.1 %scatter_custom_fusion = bf16[132,16384]{0,1:T(8,128)(2,1)} fusion(s32[8192]{0:T(1024)S(1)} %bitcast.65, bf16[8192,132]{1,0:T(8,128)(2,1)} %copy.50, bf16[]{:T(256)} %constant.85.clone.1), kind=kCustom, calls=%fused_computation.21 | custom fusion | bytes 4325888 | tf_op jit(solution)/shard_map/scatter | solution.py:40
  90.3 10.5 %copy.51 = bf16[132,8,2048]{2,0,1:T(8,128)(2,1)} copy(bf16[132,8,2048]{0,2,1:T(8,128)(2,1)} %bitcast.58) | data formatting | bytes 8650752 | tf_op jit(solution)/shard_map/all_to_all | solution.py:44
  100.9 6.0 %all-to-all-start.1 = ((bf16[132,8,2048]{2,0,1:T(8,128)(2,1)}), bf16[132,8,2048]{2,0,1:T(8,128)(2,1)}, u32[]{:S(2)}, u32[]{:S(2)}) async-start(bf16[132,8,2048]{2,0,1:T(8,128)(2,1)} %copy.51), calls=%async_computation.1 | async-start | bytes 8912896 | tf_op jit(solution)/shard_map/all_to_all | solution.py:44
  106.9 96.7 %all-to-all-done.1 = bf16[132,8,2048]{2,0,1:T(8,128)(2,1)} async-done(((bf16[132,8,2048]{2,0,1:T(8,128)(2,1)}), bf16[132,8,2048]{2,0,1:T(8,128)(2,1)}, u32[]{:S(2)}, u32[]{:S(2)}) %all-to-all-start.1) | async-done | bytes 4325408 | tf_op jit(solution)/shard_map/all_to_all | solution.py:44
  203.7 4.8 copy_convert_fusion
  209.6 10.5 %copy.72 = f32[17,8,8,2048]{3,1,2,0:T(8,128)} copy(f32[17,8,8,2048]{3,2,1,0:T(8,128)S(1)} %bitcast.56) | data formatting | bytes 17825792
  220.1 12.7 %copy.53 = f32[16384,132]{1,0:T(8,128)} copy(f32[16384,132]{0,1:T(8,128)} %bitcast.57) | data formatting | bytes 17301504 | tf_op jit(solution)/shard_map/convert_element_type | solution.py:50
  232.7 110.7 %scatter_custom_fusion.1 = f32[132,8192]{0,1:T(8,128)} fusion(s32[16384]{0:T(1024)S(1)} %bitcast.70, f32[16384,132]{1,0:T(8,128)} %copy.53, f32[]{:T(128)} %constant.80.clone.1), kind=kCustom, calls=%fused_computation.23 | custom fusion | flops 2162688 | bytes 4325888 | tf_op jit(solution)/shard_map/scatter-add | solution.py:50
  343.4 8.7 %copy.54 = f32[132,8,4,256]{3,1,2,0:T(8,128)} copy(f32[132,8,4,256]{0,3,2,1:T(8,128)} %bitcast.59) | data formatting | bytes 8650752 | tf_op jit(solution)/shard_map/reshape | solution.py:53
  352.1 3.8 add_convert_fusion
  356.0 1.9 collective-permute-start
  358.3 15.1 %collective-permute-done = bf16[132,8,1,256]{3,1,2,0:T(8,128)(2,1)S(1)} collective-permute-done((bf16[132,8,1,256]{3,1,2,0:T(8,128)(2,1)S(1)}, bf16[132,8,1,256]{3,1,2,0:T(8,128)(2,1)S(1)}, u32[]{:S(2)}, u32[]{:S(2)}) %collective-permute-start) | collective-permute-done | bytes 540704 | tf_op jit(solution)/shard_map/ppermute | solution.py:10
  375.1 1.9 collective-permute-start.1
  380.5 10.5 %collective-permute-done.1 = bf16[132,8,1,256]{3,1,2,0:T(8,128)(2,1)S(1)} collective-permute-done((bf16[132,8,1,256]{3,1,2,0:T(8,128)(2,1)}, bf16[132,8,1,256]{3,1,2,0:T(8,128)(2,1)S(1)}, u32[]{:S(2)}, u32[]{:S(2)}) %collective-permute-start.1) | collective-permute-done | bytes 540704 | tf_op jit(solution)/shard_map/ppermute | solution.py:10
  391.0 2.8 fusion.7
  395.3 3.6 all-to-all-start.2
  398.9 26.4 %all-to-all-done.2 = bf16[132,8,4,256]{3,1,0,2:T(8,128)(2,1)S(1)} async-done(((bf16[132,8,4,256]{3,1,0,2:T(8,128)(2,1)}), bf16[132,8,4,256]{3,1,0,2:T(8,128)(2,1)S(1)}, u32[]{:S(2)}, u32[]{:S(2)}) %all-to-all-start.2) | async-done | bytes 2162720 | tf_op jit(solution)/shard_map/all_to_all | solution.py:75
  425.3 2.6 convert_bitcast_fusion
  428.0 91.0 %while.18 = (s32[]{:T(128)}, bf16[132,32,1,256]{3,0,2,1:T(8,128)(2,1)S(1)}, f32[132,1,256]{2,1,0:T(1,128)S(1)}, f32[132,32,1,256]{3,1,2,0:T(8,128)}, f32[132,32]...) while((s32[]{:T(128)}, bf16[132,32,1,256]{3,0,2,1:T(8,128)(2,1)S(1)}, ...), condition=%wide.region_7.8_spmd.clone, body=%wide.region_6.7_spmd.clone.sunk | while | flops 169099 | bytes 746753 | solution.py:25
  428.7 1.9 broadcast_multiply_fusion.2
  431.6 1.9 broadcast_multiply_fusion.2
  434.4 1.9 broadcast_multiply_fusion.2
  437.3 1.9 broadcast_multiply_fusion.2
  440.1 1.9 broadcast_multiply_fusion.2
  443.0 1.9 broadcast_multiply_fusion.2
  445.8 1.9 broadcast_multiply_fusion.2
  448.7 1.9 broadcast_multiply_fusion.2
  451.5 1.9 broadcast_multiply_fusion.2
  454.3 1.9 broadcast_multiply_fusion.2
  460.0 1.9 broadcast_multiply_fusion.2
  462.9 1.9 broadcast_multiply_fusion.2
  465.7 1.9 broadcast_multiply_fusion.2
  468.6 1.9 broadcast_multiply_fusion.2
  477.1 1.9 broadcast_multiply_fusion.2
  479.9 1.9 broadcast_multiply_fusion.2
  482.8 1.9 broadcast_multiply_fusion.2
  485.6 1.9 broadcast_multiply_fusion.2
  497.0 1.9 broadcast_multiply_fusion.2
  499.9 1.9 broadcast_multiply_fusion.2
  502.7 1.9 broadcast_multiply_fusion.2
  514.1 1.9 broadcast_multiply_fusion.2
  516.9 1.9 broadcast_multiply_fusion.2
  519.0 29.6 %all_to_all.45 = bf16[132,32,1,256]{3,0,2,1:T(8,128)(2,1)S(1)} all-to-all(bf16[132,32,1,256]{3,0,2,1:T(8,128)(2,1)S(1)} %get-tuple-element.137), channel_id=1, replica_groups=mesh['xy'=8,'gz'=4] {'gz'}, dimensions={1} | all-to-all | bytes 4325376 | tf_op jit(solution)/shard_map/all_to_all | solution.py:78
  548.6 3.0 copy.65
  (174 shorter events, 60.4 us)
Async XLA Ops:
  38.6 62.3 %all-to-all-start = ((s32[1,8,2048]{2,0,1:T(1,128)}), s32[1,8,2048]{2,0,1:T(1,128)S(1)}, u32[]{:S(2)}, u32[]{:S(2)}) async-start(s32[1,8,2048]{2,0,1:T(1,128)} %bitcast.4), calls=%async_computation | async-start | bytes 131072 | tf_op jit(solution)/shard_map/all_to_all | solution.py:45
  100.9 102.8 %all-to-all-start.1 = ((bf16[132,8,2048]{2,0,1:T(8,128)(2,1)}), bf16[132,8,2048]{2,0,1:T(8,128)(2,1)}, u32[]{:S(2)}, u32[]{:S(2)}) async-start(bf16[132,8,2048]{2,0,1:T(8,128)(2,1)} %copy.51), calls=%async_computation.1 | async-start | bytes 8912896 | tf_op jit(solution)/shard_map/all_to_all | solution.py:44
  352.1 5.8 %copy-start = (bf16[8,4,256]{2,1,0:T(4,128)(2,1)S(1)}, bf16[8,4,256]{2,1,0:T(4,128)(2,1)}, u32[]{:S(2)}) copy-start(bf16[8,4,256]{2,1,0:T(4,128)(2,1)} %param.13) | copy-start | bytes 49156
  352.1 5.9 %copy-start.1 = (bf16[8,4,256]{2,1,0:T(4,128)(2,1)S(1)}, bf16[8,4,256]{2,1,0:T(4,128)(2,1)}, u32[]{:S(2)}) copy-start(bf16[8,4,256]{2,1,0:T(4,128)(2,1)} %param.14) | copy-start | bytes 49156
  356.0 17.3 %collective-permute-start = (bf16[132,8,1,256]{3,1,2,0:T(8,128)(2,1)S(1)}, bf16[132,8,1,256]{3,1,2,0:T(8,128)(2,1)S(1)}, u32[]{:S(2)}, u32[]{:S(2)}) collective-permute-start(bf16[132,8,1,256]{3,1,2,0:T(8,128)(2,1)S(1)} %slice.34), channel_id=1, source_target_pairs={{0,4},{4,8},{8,12},{12,16},{16,20},{20,24},{24,28},{1,5},{5,9},{9,... | collective-permute-start | bytes 1622024 | tf_op jit(solution)/shard_map/ppermute | solution.py:10
  375.1 15.8 %collective-permute-start.1 = (bf16[132,8,1,256]{3,1,2,0:T(8,128)(2,1)}, bf16[132,8,1,256]{3,1,2,0:T(8,128)(2,1)S(1)}, u32[]{:S(2)}, u32[]{:S(2)}) collective-permute-start(bf16[132,8,1,256]{3,1,2,0:T(8,128)(2,1)} %slice.48), channel_id=1, source_target_pairs={{4,0},{8,4},{12,8},{16,12},{20,16},{24,20},{28,24},{5,1},{9,5},{13... | collective-permute-start | bytes 1622024 | tf_op jit(solution)/shard_map/ppermute | solution.py:10
  395.3 30.0 %all-to-all-start.2 = ((bf16[132,8,4,256]{3,1,0,2:T(8,128)(2,1)}), bf16[132,8,4,256]{3,1,0,2:T(8,128)(2,1)S(1)}, u32[]{:S(2)}, u32[]{:S(2)}) async-start(bf16[132,8,4,256]{3,1,0,2:T(8,128)(2,1)} %copy.59), calls=%async_computation.2 | async-start | bytes 4325376 | tf_op jit(solution)/shard_map/all_to_all | solution.py:75
where the time goes:
time: 555 us; the launch traced here: 552 us
  other arithmetic  194 us (35%)
  local copies, waits for them, and re-layouts  158 us (28%)
  waiting for transfers between devices  149 us (27%)
  blocking collectives  29.6 us (5%)
  starting transfers between devices  19.5 us (4%)
    scatter-add x1, other arithmetic, per_device(): summed = jnp.zeros((comps, slab_levels * xcells * ycells), jnp.float32).a...  111 us
    all_to_all x1, waiting for transfers between devices, per_device(): lax.all_to_all(packed, 'xy', split_axis=1, concat_axis=1, tiled=True)  96.7 us
    mul x32, other arithmetic, descend(): return (output, courant * value)  59.3 us
    unnamed x8, local copies, waits for them, and re-layouts  48.4 us
    scatter x1, local copies, waits for them, and re-layouts, per_device(): jnp.zeros((comps, peer_count * capacity), jnp.bfloat16).at[:, slot_index]  40.1 us
    all_to_all x1, blocking collectives, per_device(): lax.all_to_all(output.astype(jnp.bfloat16), 'gz', split_axis=1, concat_ax...  29.6 us
    all_to_all x1, waiting for transfers between devices, per_device(): lax.all_to_all(advected, 'gz', split_axis=2, concat_axis=1, tiled=True)  26.4 us
    ppermute x2, waiting for transfers between devices, shifted(): lax.ppermute(value, axis, [(source, source + steps) for source in range(f...  25.5 us
  transfers between devices with their start and end apart: 5, of which 4 were waited for; matrix products, arithmetic and copies ran while one was open for 11% of the time, Pallas kernels for 0%

commit v1 on v0

v1 whole, which is shorter than its diff:
```python
import functools

import jax
import jax.numpy as jnp
from jax import lax
from jax.experimental import pallas as pl
from jax.experimental.pallas import tpu as pltpu
from jax.sharding import PartitionSpec as P

MESH = pl.DeviceIdType.MESH
NT = (((1,), (1,)), ((), ()))


def up(value, multiple):
    return -(-value // multiple) * multiple


def running_counts(member):
    tiles, count = member.shape
    run = 128
    grouped = member.astype(jnp.bfloat16).reshape(tiles * (count // run), run)
    inside = jnp.dot(
        grouped, jnp.triu(jnp.ones((run, run), jnp.bfloat16)), preferred_element_type=jnp.float32
    ).reshape(tiles, count // run, run)
    before = jnp.dot(
        inside[:, :, run - 1].astype(jnp.bfloat16),
        jnp.triu(jnp.ones((count // run, count // run), jnp.bfloat16), 1),
        preferred_element_type=jnp.float32,
    )
    return (inside + before[:, :, None]).reshape(tiles, count).astype(jnp.int32)


def pack_kernel(block, starts_ref, rows_ref, slot_ref, out_ref):
    peers, height, capacity = out_ref.shape
    width = min(256, capacity)
    blocks = rows_ref.shape[1] // block
    window = lax.broadcasted_iota(jnp.int32, (width, block), 0)

    def clear(tile, carry):
        out_ref[tile] = jnp.zeros((height, capacity), out_ref.dtype)
        return carry

    lax.fori_loop(0, peers, clear, 0)

    def step(counter, carry):
        part, tile = counter // peers, counter % peers
        columns = pl.ds(pl.multiple_of(part * block, block), block)
        first = starts_ref[tile, part]
        last = starts_ref[tile, part + 1]

        def place(chunk, inner):
            base = tile * capacity + chunk * width
            match = jnp.where(window == slot_ref[:, columns] - base, 1.0, 0.0).astype(jnp.bfloat16)
            moved = lax.dot_general(
                rows_ref[:, columns], match, NT, preferred_element_type=jnp.float32
            )
            spot = pl.ds(pl.multiple_of(chunk * width, width), width)
            out_ref[tile, :, spot] += moved.astype(out_ref.dtype)
            return inner

        stop = jnp.where(last > first, (last - 1) // width + 1, first // width)
        lax.fori_loop(first // width, stop, place, 0)
        return carry

    lax.fori_loop(0, blocks * peers, step, 0)


def main_kernel(
    comps, packed, base, cx, cy, scale, gain, out, arrived, total, updated, advected, left, right,
    next_cx, flow, inflow, send_sem, recv_sem, halo_send, halo_recv, flow_send, flow_recv,
):
    peers, height, capacity = packed.shape
    xcells, levels, _, width = updated.shape
    slabs = lax.axis_size("gz")
    me, slab = lax.axis_index("xy"), lax.axis_index("gz")
    has_prev, has_next = me > 0, me < peers - 1
    has_below, has_above = slab > 0, slab < slabs - 1
    groups = xcells * levels

    barrier = pltpu.get_barrier_semaphore()

    def greet(step, carry):
        pl.semaphore_signal(
            barrier, inc=1, device_id=((me + step) % peers, slab), device_id_type=MESH
        )
        return carry

    lax.fori_loop(1, peers, greet, 0)

    @pl.when(has_below)
    def _():
        pl.semaphore_signal(barrier, inc=1, device_id=(me, slab - 1), device_id_type=MESH)

    @pl.when(has_above)
    def _():
        pl.semaphore_signal(barrier, inc=1, device_id=(me, slab + 1), device_id_type=MESH)

    greeted = jnp.where(has_below, 1, 0) + jnp.where(has_above, 1, 0)
    pl.semaphore_wait(barrier, peers - 1 + greeted)

    def row_copy(step):
        target = (me + step) % peers
        return pltpu.make_async_remote_copy(
            src_ref=packed.at[target],
            dst_ref=arrived.at[step],
            send_sem=send_sem.at[step],
            recv_sem=recv_sem.at[step],
            device_id=(target, slab),
            device_id_type=MESH,
        )

    def start_rows(step, carry):
        row_copy(step).start()
        return carry

    lax.fori_loop(1, peers, start_rows, 0)

    depth = min(512, capacity)
    bundle = 8
    lane_cells = lax.broadcasted_iota(jnp.int32, (width, depth), 0).astype(jnp.float32)

    def clear(group, carry):
        total[group] = jnp.zeros((height, width), jnp.float32)
        return carry

    lax.fori_loop(0, groups, clear, 0)

    def add_rows(source, at):
        def part(index, carry):
            columns = pl.ds(pl.multiple_of(index * depth, depth), depth)
            block = source[at, :, columns]
            tags = block[comps // 16 * 16 :, :].astype(jnp.float32)
            low = tags[comps % 16 : comps % 16 + 1]
            high = tags[comps % 16 + 1 : comps % 16 + 2]
            match = jnp.where(lane_cells == low, 1.0, 0.0).astype(jnp.bfloat16)

            def product(group, inner):
                first = group * bundle
                masks = [
                    jnp.where(high == (first + n).astype(jnp.float32), 1.0, 0.0).astype(jnp.bfloat16)
                    for n in range(bundle)
                ]
                rows = jnp.concatenate([block * mask for mask in masks], axis=0)
                sums = lax.dot_general(rows, match, NT, preferred_element_type=jnp.float32)
                total[pl.ds(first, bundle)] += sums.reshape(bundle, height, width)
                return inner

            lax.fori_loop(0, groups // bundle, product, 0)
            return carry

        lax.fori_loop(0, capacity // depth, part, 0)

    add_rows(packed, me)

    def receive(step, carry):
        row_copy(step).wait_recv()
        add_rows(arrived, step)
        return carry

    lax.fori_loop(1, peers, receive, 0)

    def finish(group, carry):
        value = base[group].astype(jnp.float32) + total[group]
        updated[group % xcells, group // xcells] = value.astype(jnp.bfloat16)
        return carry

    lax.fori_loop(0, groups, finish, 0)

    def halo_copy(which, source, target, step):
        return pltpu.make_async_remote_copy(
            src_ref=source,
            dst_ref=target,
            send_sem=halo_send.at[which],
            recv_sem=halo_recv.at[which],
            device_id=((me + step + peers) % peers, slab),
            device_id_type=MESH,
        )

    to_next = halo_copy(0, updated.at[xcells - 1], left, 1)
    to_prev = halo_copy(1, updated.at[0], right, -1)
    face_to_prev = halo_copy(2, cx.at[0], next_cx, -1)

    @pl.when(has_next)
    def _():
        to_next.start()

    @pl.when(has_prev)
    def _():
        to_prev.start()
        face_to_prev.start()

    @pl.when(jnp.logical_not(has_prev))
    def _():
        left[...] = jnp.zeros_like(left)

    @pl.when(jnp.logical_not(has_next))
    def _():
        right[...] = jnp.zeros_like(right)
        next_cx[...] = jnp.zeros_like(next_cx)

    def flow_copy(i):
        return pltpu.make_async_remote_copy(
            src_ref=flow.at[i],
            dst_ref=inflow.at[i],
            send_sem=flow_send.at[i],
            recv_sem=flow_recv.at[i],
            device_id=(me, (slab + slabs - 1) % slabs),
            device_id_type=MESH,
        )

    reach = gain[0]
    for k in range(1, levels):
        reach = reach * gain[k]

    def advect(i):
        def level(counter, current_flow):
            k = levels - 1 - counter
            row = pl.ds(k, 1)
            current = updated[i, k].astype(jnp.float32)
            before = (left[k] if i == 0 else updated[i - 1, k]).astype(jnp.float32)
            after = (right[k] if i == xcells - 1 else updated[i + 1, k]).astype(jnp.float32)
            west = cx[i, row]
            east = next_cx[row] if i == xcells - 1 else cx[i + 1, row]
            south = cy[i, row]
            flux_west = jnp.maximum(west, 0.0) * before + jnp.minimum(west, 0.0) * current
            flux_east = jnp.maximum(east, 0.0) * current + jnp.minimum(east, 0.0) * after
            below = pltpu.roll(current, 1, 1)
            flux_south = jnp.maximum(south, 0.0) * below + jnp.minimum(south, 0.0) * current
            flux_north = pltpu.roll(flux_south, width - 1, 1)
            value = current - (flux_east - flux_west) - (flux_north - flux_south)
            value = value.astype(jnp.bfloat16)
            advected[i, k] = value
            return (value.astype(jnp.float32) + current_flow) * gain[k]

        flow[i] = lax.fori_loop(0, levels, level, jnp.zeros((height, width), jnp.float32))

    def chain(i):
        @pl.when(has_above)
        def _():
            flow_copy(i).wait_recv()
            flow[i] += reach * inflow[i]

        @pl.when(jnp.logical_not(has_above))
        def _():
            inflow[i] = jnp.zeros((height, width), jnp.float32)

        @pl.when(has_below)
        def _():
            flow_copy(i).start()

    for i in range(1, xcells - 1):
        advect(i)

    @pl.when(has_prev)
    def _():
        to_next.wait_recv()

    @pl.when(has_next)
    def _():
        to_prev.wait_recv()
        face_to_prev.wait_recv()

    for i in range(1, xcells - 1):
        chain(i)
    for i in (0, xcells - 1):
        advect(i)
        chain(i)

    for i in [*range(1, xcells - 1), 0, xcells - 1]:

        def settle(counter, current):
            k = levels - 1 - counter
            value = (advected[i, k].astype(jnp.float32) + current) * scale[k]
            out[k * xcells + i] = value.astype(jnp.bfloat16)
            return (advected[i, k].astype(jnp.float32) + current) * gain[k]

        lax.fori_loop(0, levels, settle, inflow[i])

    def sent(step, carry):
        row_copy(step).wait_send()
        return carry

    lax.fori_loop(1, peers, sent, 0)

    @pl.when(has_next)
    def _():
        to_next.wait_send()

    @pl.when(has_prev)
    def _():
        to_prev.wait_send()
        face_to_prev.wait_send()

    @pl.when(has_below)
    def _():
        for i in range(xcells):
            flow_copy(i).wait_send()


def per_device(base_field, increments, dest_tile, dest_cell, courant_x, courant_y, fall_courant):
    comps, levels, xcells, ycells = base_field.shape
    row_count = increments.shape[1]
    peers = lax.axis_size("xy")
    capacity = 2 * row_count // peers
    height = up(comps + 2, 16)
    groups = levels * xcells
    block = 512

    targets = dest_tile[:, 0]
    member = (targets[None, :] == jnp.arange(peers, dtype=jnp.int32)[:, None]).astype(jnp.int32)
    counts = running_counts(member)
    slots = targets * capacity + jnp.sum(counts * member, axis=0) - 1
    starts = jnp.pad(counts[:, block - 1 :: block], ((0, 0), (1, 0)))
    low = (dest_cell % ycells).astype(jnp.bfloat16)
    high = (dest_cell // ycells).astype(jnp.bfloat16)
    rows = jnp.concatenate(
        [
            increments,
            low[None],
            high[None],
            jnp.zeros((height - comps - 2, row_count), jnp.bfloat16),
        ],
        axis=0,
    )
    vmem = pl.BlockSpec(memory_space=pltpu.VMEM)
    packed = pl.pallas_call(
        functools.partial(pack_kernel, block),
        out_shape=jax.ShapeDtypeStruct((peers, height, capacity), jnp.bfloat16),
        in_specs=[pl.BlockSpec(memory_space=pltpu.SMEM), vmem, vmem],
        out_specs=vmem,
        compiler_params=pltpu.CompilerParams(vmem_limit_bytes=48 * 2**20),
        name="pack_rows",
    )(starts, rows, slots[None])

    pad_comps = ((0, 0), (0, height - comps), (0, 0))
    base = jnp.pad(
        jnp.transpose(base_field, (1, 2, 0, 3)).reshape(groups, comps, ycells), pad_comps
    )
    first = jnp.logical_and(
        lax.axis_index("xy") == 0, jnp.arange(xcells)[:, None, None] == 0
    )
    face_x = jnp.where(first, 0.0, jnp.transpose(courant_x.astype(jnp.float32), (1, 0, 2)))
    face_y = jnp.transpose(courant_y.astype(jnp.float32), (1, 0, 2))
    face_y = jnp.where(jnp.arange(ycells)[None, None, :] == 0, 0.0, face_y)
    fall = lax.dynamic_slice_in_dim(fall_courant, lax.axis_index("gz") * levels, levels, 1)
    fall = jnp.pad(jnp.transpose(fall)[:, :, None], pad_comps)
    scale = 1.0 / (1.0 + fall)
    gain = fall / (1.0 + fall)

    settled = pl.pallas_call(
        functools.partial(main_kernel, comps),
        out_shape=jax.ShapeDtypeStruct((groups, height, ycells), jnp.bfloat16),
        in_specs=[vmem] * 6,
        out_specs=vmem,
        scratch_shapes=[
            pltpu.VMEM((peers, height, capacity), jnp.bfloat16),
            pltpu.VMEM((groups, height, ycells), jnp.float32),
            pltpu.VMEM((xcells, levels, height, ycells), jnp.bfloat16),
            pltpu.VMEM((xcells, levels, height, ycells), jnp.bfloat16),
            pltpu.VMEM((levels, height, ycells), jnp.bfloat16),
            pltpu.VMEM((levels, height, ycells), jnp.bfloat16),
            pltpu.VMEM((levels, ycells), jnp.float32),
            pltpu.VMEM((xcells, height, ycells), jnp.float32),
            pltpu.VMEM((xcells, height, ycells), jnp.float32),
            pltpu.SemaphoreType.DMA((peers,)),
            pltpu.SemaphoreType.DMA((peers,)),
            pltpu.SemaphoreType.DMA((3,)),
            pltpu.SemaphoreType.DMA((3,)),
            pltpu.SemaphoreType.DMA((xcells,)),
            pltpu.SemaphoreType.DMA((xcells,)),
        ],
        compiler_params=pltpu.CompilerParams(
            vmem_limit_bytes=56 * 2**20, collective_id=0, has_side_effects=True
        ),
        name="exchange_advect_settle",
    )(packed, base, face_x, face_y, scale, gain)
    settled = settled.reshape(levels, xcells, height, ycells)[:, :, :comps]
    return jnp.transpose(settled, (2, 0, 1, 3))


def solution(mesh):
    in_specs = (
        P(None, "gz", "xy", None),
        P(None, ("xy", "gz")),
        P(("xy", "gz"), None),
        P(("xy", "gz")),
        P("gz", "xy", None),
        P("gz", "xy", None),
        P(),
    )
    out_specs = P(None, "gz", "xy", None)
    return jax.shard_map(
        per_device, mesh=mesh, in_specs=in_specs, out_specs=out_specs, check_vma=False
    )
```

time: 555 us -> 232 us (0.42)
  Pallas kernels: 0 us -> 215 us
  other arithmetic: 194 us -> 6.71 us
  local copies, waits for them, and re-layouts: 158 us -> 8.12 us
  waiting for transfers between devices: 149 us -> 0 us
  blocking collectives: 29.6 us -> 0 us
  starting transfers between devices: 19.5 us -> 0 us
    pallas_call x0 -> x2, Pallas kernels: none -> 215 us  [the longest x1 172 us: per_device(): pl.pallas_call(functools.partial(main_kernel, comps), out_shape=jax.Shape...]
    all_to_all x3 -> x0, waiting for transfers between devices: 123 us -> none  [the longest x1 96.7 us: per_device(): lax.all_to_all(packed, 'xy', split_axis=1, concat_axis=1, tiled=True)]
    scatter-add x1 -> x0, other arithmetic: 111 us -> none  [per_device(): summed = jnp.zeros((comps, slab_levels * xcells * ycells), jnp.float32).a...]
    mul x32 -> x0, other arithmetic: 59.3 us -> none  [descend(): return (output, courant * value)]
    unnamed x8 -> x10, local copies, waits for them, and re-layouts: 48.4 us -> 2.75 us
    scatter x1 -> x0, local copies, waits for them, and re-layouts: 40.1 us -> none  [per_device(): jnp.zeros((comps, peer_count * capacity), jnp.bfloat16).at[:, slot_index]]
    all_to_all x1 -> x0, blocking collectives: 29.6 us -> none  [per_device(): lax.all_to_all(output.astype(jnp.bfloat16), 'gz', split_axis=1, concat_ax...]
    ppermute x2 -> x0, waiting for transfers between devices: 25.5 us -> none  [shifted(): lax.ppermute(value, axis, [(source, source + steps) for source in range(f...]
  transfers between devices with their start and end apart: 5 -> 0, of which waited for: 4 -> 0; matrix products, arithmetic and copies ran while one was open for 11% -> 0% of each run, Pallas kernels for 0% -> 0%
where the time goes in v1:
time: 232 us; the launch traced here: 231 us
  Pallas kernels  215 us (93%)
  local copies, waits for them, and re-layouts  8.12 us (3%)
  other arithmetic  6.71 us (3%)
    pallas_call x1, Pallas kernels, per_device(): pl.pallas_call(functools.partial(main_kernel, comps), out_shape=jax.Shape...  172 us
    pallas_call x1, Pallas kernels, per_device(): pl.pallas_call(functools.partial(pack_kernel, block), out_shape=jax.Shape...  43.3 us

profile of v1, /device:TPU:24, one launch (start us, length us, event | category | flops | bytes accessed | tf_op | source)
XLA Modules:
  0.0 231.2 jit_solution(13918815806431332526)
XLA Ops:
  0.0 0.0 copy-start
  0.0 1.0 fusion
  1.0 0.2 fusion.1
  1.3 0.1 fusion.13
  1.4 0.9 select_reduce_fusion
  2.3 0.8 fusion.8.slot_ref
  3.1 0.1 convert_bitcast_fusion
  3.2 0.2 copy.31
  3.4 0.1 slice.11
  3.5 0.1 pad.12.starts_ref
  3.6 0.8 fusion.4
  4.4 0.1 pad.18.clone
  4.5 2.3 maximum_maximum_fusion.rows_ref
  6.8 43.3 %pack_rows.1.packed = bf16[8,144,2048]{2,1,0:T(8,128)(2,1)} custom-call(s32[8,17]{1,0:T(8,128)S(1)} %pad.12.starts_ref, bf16[144,8192]{1,0:T(8,128)(2,1)S(1)} %maximum_maximum_fusion.rows_ref, s32[1,8192]{1,0:T(1,128)S(1)} %fusion.8.slot_ref), custom_call_target="tpu_custom_call" | custom-call | tf_op jit(solution)/shard_map/pack_rows/pallas_call | solution.py:326
  50.1 0.0 copy-start.2
  50.1 0.0 copy-start.3
  50.1 0.0 copy-start.1
  50.1 0.0 copy-done
  50.1 0.2 copy.20
  50.4 1.1 add_divide_fusion
  51.5 0.0 copy-done.2
  51.5 0.0 copy-done.3
  51.5 0.7 select_bitcast_fusion
  52.2 0.0 copy-done.1
  52.2 1.2 copy.17
  53.4 1.6 pad.13.base
  55.0 171.9 %exchange_advect_settle.1 = bf16[32,144,256]{2,1,0:T(8,128)(2,1)} custom-call(bf16[8,144,2048]{2,1,0:T(8,128)(2,1)} %pack_rows.1.packed, bf16[32,144,256]{2,1,0:T(8,128)(2,1)} %pad.13.base, f32[4,8,256]{2,1,0:T(8,128)} %get-tuple-element.10.cx, f32[4,8,256]{2,1,0:T(8,128)} %get-tuple-element.9.cy, f32[8,144,1]{2,1,0:T(8,128)} %get-tuple-element.6.scale, ...), custom_call_target="tpu_custom_call" | custom-call | tf_op jit(solution)/shard_map/exchange_advect_settle/pallas_call | solution.py:350
  226.9 1.8 slice.14
  228.7 2.6 %copy.30 = bf16[8,4,132,256]{3,1,0,2:T(4,128)(2,1)} copy(bf16[8,4,132,256]{3,2,1,0:T(8,128)(2,1)S(1)} %slice.14) | data formatting | bytes 4325376
  (7 shorter events, 0.1 us)
Async XLA Ops:
  0.0 50.1 %copy-start = (f32[132,32]{0,1:T(8,128)S(1)}, f32[132,32]{0,1:T(8,128)}, u32[]{:S(2)}) copy-start(f32[132,32]{0,1:T(8,128)} %param.13) | copy-start | bytes 50692
  50.1 1.4 copy-start.2
  50.1 1.4 copy-start.3
  50.1 2.1 copy-start.1

commit v2 on v1

--- a/solution.py
+++ b/solution.py
@@ -42,27 +42,47 @@
 
     lax.fori_loop(0, peers, clear, 0)
 
+    bundle = min(8, peers)
+    windows = capacity // width
+
     def step(counter, carry):
-        part, tile = counter // peers, counter % peers
+        part, first_tile = counter // (peers // bundle), counter % (peers // bundle) * bundle
         columns = pl.ds(pl.multiple_of(part * block, block), block)
-        first = starts_ref[tile, part]
-        last = starts_ref[tile, part + 1]
-
-        def place(chunk, inner):
+        slots = slot_ref[:, columns]
+
+        def match(tile, chunk):
             base = tile * capacity + chunk * width
-            match = jnp.where(window == slot_ref[:, columns] - base, 1.0, 0.0).astype(jnp.bfloat16)
-            moved = lax.dot_general(
-                rows_ref[:, columns], match, NT, preferred_element_type=jnp.float32
-            )
-            spot = pl.ds(pl.multiple_of(chunk * width, width), width)
-            out_ref[tile, :, spot] += moved.astype(out_ref.dtype)
+            return jnp.where(window == slots - base, 1.0, 0.0).astype(jnp.bfloat16)
+
+        def move(matches):
+            return lax.dot_general(
+                rows_ref[:, columns], matches, NT, preferred_element_type=jnp.float32
+            ).astype(out_ref.dtype)
+
+        def spot(chunk):
+            return pl.ds(pl.multiple_of(chunk * width, width), width)
+
+        tiles = [first_tile + n for n in range(bundle)]
+        chunks = [jnp.minimum(starts_ref[tile, part] // width, windows - 1) for tile in tiles]
+        moved = move(jnp.concatenate([match(*pair) for pair in zip(tiles, chunks)], axis=0))
+        for n in range(bundle):
+            out_ref[tiles[n], :, spot(chunks[n])] += moved[:, n * width : (n + 1) * width]
+
+        def more(tile, inner):
+            start = starts_ref[tile, part]
+            stop = starts_ref[tile, part + 1]
+
+            def place(chunk, innermost):
+                out_ref[tile, :, spot(chunk)] += move(match(tile, chunk))
+                return innermost
+
+            lax.fori_loop(start // width + 1, (stop + width - 1) // width, place, 0)
             return inner
 
-        stop = jnp.where(last > first, (last - 1) // width + 1, first // width)
-        lax.fori_loop(first // width, stop, place, 0)
-        return carry
-
-    lax.fori_loop(0, blocks * peers, step, 0)
+        lax.fori_loop(first_tile, first_tile + bundle, more, 0)
+        return carry
+
+    lax.fori_loop(0, blocks * (peers // bundle), step, 0)
 
 
 def main_kernel(
@@ -121,6 +141,10 @@
 
     def clear(group, carry):
         total[group] = jnp.zeros((height, width), jnp.float32)
+        tail = comps // 16 * 16
+        updated[group % xcells, group // xcells, tail:, :] = jnp.zeros(
+            (height - tail, width), jnp.bfloat16
+        )
         return carry
 
     lax.fori_loop(0, groups, clear, 0)
@@ -160,8 +184,8 @@
     lax.fori_loop(1, peers, receive, 0)
 
     def finish(group, carry):
-        value = base[group].astype(jnp.float32) + total[group]
-        updated[group % xcells, group // xcells] = value.astype(jnp.bfloat16)
+        value = base[group].astype(jnp.float32) + total[group, :comps]
+        updated[group % xcells, group // xcells, :comps] = value.astype(jnp.bfloat16)
         return carry
 
     lax.fori_loop(0, groups, finish, 0)
@@ -271,7 +295,7 @@
         def settle(counter, current):
             k = levels - 1 - counter
             value = (advected[i, k].astype(jnp.float32) + current) * scale[k]
-            out[k * xcells + i] = value.astype(jnp.bfloat16)
+            out[k * xcells + i] = value[:comps].astype(jnp.bfloat16)
             return (advected[i, k].astype(jnp.float32) + current) * gain[k]
 
         lax.fori_loop(0, levels, settle, inflow[i])
@@ -333,9 +357,7 @@
     )(starts, rows, slots[None])
 
     pad_comps = ((0, 0), (0, height - comps), (0, 0))
-    base = jnp.pad(
-        jnp.transpose(base_field, (1, 2, 0, 3)).reshape(groups, comps, ycells), pad_comps
-    )
+    base = jnp.transpose(base_field, (1, 2, 0, 3)).reshape(groups, comps, ycells)
     first = jnp.logical_and(
         lax.axis_index("xy") == 0, jnp.arange(xcells)[:, None, None] == 0
     )
@@ -349,7 +371,7 @@
 
     settled = pl.pallas_call(
         functools.partial(main_kernel, comps),
-        out_shape=jax.ShapeDtypeStruct((groups, height, ycells), jnp.bfloat16),
+        out_shape=jax.ShapeDtypeStruct((groups, comps, ycells), jnp.bfloat16),
         in_specs=[vmem] * 6,
         out_specs=vmem,
         scratch_shapes=[
@@ -374,7 +396,7 @@
         ),
         name="exchange_advect_settle",
     )(packed, base, face_x, face_y, scale, gain)
-    settled = settled.reshape(levels, xcells, height, ycells)[:, :, :comps]
+    settled = settled.reshape(levels, xcells, comps, ycells)
     return jnp.transpose(settled, (2, 0, 1, 3))
 
 

time: 232 us -> 214 us (0.922)
  Pallas kernels: 215 us -> 198 us
    pallas_call x1, Pallas kernels: 43.3 us -> 26.2 us  [per_device(): pl.pallas_call(functools.partial(pack_kernel, block), out_shape=jax.Shape...]
    reshape x0 -> x1, local copies, waits for them, and re-layouts: none -> 4.21 us  [per_device(): settled = settled.reshape(levels, xcells, comps, ycells)]
    unnamed x10 -> x9, local copies, waits for them, and re-layouts: 2.75 us -> 0.17 us
where the time goes in v2:
time: 214 us
  Pallas kernels  198 us (93%)
  local copies, waits for them, and re-layouts  7.79 us (4%)
  other arithmetic  6.72 us (3%)
    pallas_call x1, Pallas kernels, per_device(): pl.pallas_call(functools.partial(main_kernel, comps), out_shape=jax.Shape...  172 us
    pallas_call x1, Pallas kernels, per_device(): pl.pallas_call(functools.partial(pack_kernel, block), out_shape=jax.Shape...  26.2 us

profile of v2, /device:TPU:24, one launch (start us, length us, event | category | flops | bytes accessed | tf_op | source)
XLA Modules:
  0.0 213.7 jit_solution(11881480901903615525)
XLA Ops:
  0.0 0.0 copy-start
  0.0 1.0 fusion
  1.0 0.2 fusion.1
  1.3 0.1 fusion.13
  1.4 0.9 select_reduce_fusion
  2.3 0.8 fusion.8.slot_ref
  3.1 0.1 convert_bitcast_fusion
  3.2 0.2 copy.30
  3.4 0.1 slice.8
  3.5 0.1 pad.8.starts_ref
  3.6 0.8 fusion.4
  4.4 0.1 pad.13.clone
  4.5 2.3 %maximum_maximum_fusion.rows_ref = bf16[144,8192]{1,0:T(8,128)(2,1)S(1)} fusion(bf16[1,8192]{1,0:T(2,128)(2,1)S(1)} %broadcast_in_dim.58, bf16[1,8192]{1,0:T(2,128)(2,1)S(1)} %broadcast_in_dim.57, bf16[132,8192]{1,0:T(8,128)(2,1)} %param.8, bf16[144]{0:T(256)(128)(2,1)S(1)} %pad.13.clone), kind=kLoop, calls=%fused_computation | loop fusion | flops 9437184 | bytes 4555040 | tf_op jit(solution)/shard_map/concatenate | solution.py:340
  6.8 26.2 %pack_rows.1.packed = bf16[8,144,2048]{2,1,0:T(8,128)(2,1)} custom-call(s32[8,17]{1,0:T(8,128)S(1)} %pad.8.starts_ref, bf16[144,8192]{1,0:T(8,128)(2,1)S(1)} %maximum_maximum_fusion.rows_ref, s32[1,8192]{1,0:T(1,128)S(1)} %fusion.8.slot_ref), custom_call_target="tpu_custom_call" | custom-call | tf_op jit(solution)/shard_map/pack_rows/pallas_call | solution.py:350
  33.0 0.0 copy-start.2
  33.0 0.0 copy-start.3
  33.0 0.0 copy-start.1
  33.0 0.0 copy-done
  33.0 0.2 copy.20
  33.2 1.1 add_divide_fusion
  34.3 0.0 copy-done.2
  34.4 0.0 copy-done.3
  34.4 0.7 select_bitcast_fusion
  35.1 0.0 copy-done.1
  35.1 2.6 %copy.17 = bf16[8,4,132,256]{3,2,1,0:T(8,128)(2,1)} copy(bf16[8,4,132,256]{3,1,0,2:T(4,128)(2,1)S(1)} %bitcast.31) | data formatting | bytes 4325376 | tf_op jit(solution)/shard_map/transpose | solution.py:360
  37.7 171.8 %exchange_advect_settle.1 = bf16[32,132,256]{2,1,0:T(8,128)(2,1)} custom-call(bf16[8,144,2048]{2,1,0:T(8,128)(2,1)} %pack_rows.1.packed, bf16[32,132,256]{2,1,0:T(8,128)(2,1)} %bitcast.30, f32[4,8,256]{2,1,0:T(8,128)} %get-tuple-element.10.cx, f32[4,8,256]{2,1,0:T(8,128)} %get-tuple-element.9.cy, f32[8,144,1]{2,1,0:T(8,128)} %get-tuple-element.6.scale, ...), custom_call_target="tpu_custom_call" | custom-call | tf_op jit(solution)/shard_map/exchange_advect_settle/pallas_call | solution.py:372
  209.5 4.2 %copy.29 = bf16[8,4,132,256]{3,1,0,2:T(4,128)(2,1)} copy(bf16[8,4,132,256]{3,2,1,0:T(8,128)(2,1)} %bitcast.29) | data formatting | bytes 4325376 | tf_op jit(solution)/shard_map/reshape | solution.py:399
  (7 shorter events, 0.1 us)
Async XLA Ops:
  0.0 33.0 %copy-start = (f32[132,32]{0,1:T(8,128)S(1)}, f32[132,32]{0,1:T(8,128)}, u32[]{:S(2)}) copy-start(f32[132,32]{0,1:T(8,128)} %param.13) | copy-start | bytes 50692
  33.0 1.4 copy-start.2
  33.0 1.4 copy-start.3
  33.0 2.1 copy-start.1

commit v3 on v2

--- a/solution.py
+++ b/solution.py
@@ -135,7 +135,7 @@
 
     lax.fori_loop(1, peers, start_rows, 0)
 
-    depth = min(512, capacity)
+    depth = min(1024, capacity)
     bundle = 8
     lane_cells = lax.broadcasted_iota(jnp.int32, (width, depth), 0).astype(jnp.float32)
 

time: 214 us -> 207 us (0.967)
  Pallas kernels: 198 us -> 191 us
    pallas_call x1, Pallas kernels: 172 us -> 165 us  [per_device(): pl.pallas_call(functools.partial(main_kernel, comps), out_shape=jax.Shape...]
where the time goes in v3:
time: 207 us
  Pallas kernels  191 us (92%)
  local copies, waits for them, and re-layouts  7.79 us (4%)
  other arithmetic  6.72 us (3%)
    pallas_call x1, Pallas kernels, per_device(): pl.pallas_call(functools.partial(main_kernel, comps), out_shape=jax.Shape...  165 us
    pallas_call x1, Pallas kernels, per_device(): pl.pallas_call(functools.partial(pack_kernel, block), out_shape=jax.Shape...  25.9 us
    reshape x1, local copies, waits for them, and re-layouts, per_device(): settled = settled.reshape(levels, xcells, comps, ycells)  4.21 us

profile of v3, /device:TPU:24, one launch (start us, length us, event | category | flops | bytes accessed | tf_op | source)
XLA Modules:
  0.0 206.5 jit_solution(6625194322817080471)
XLA Ops:
  0.0 0.0 copy-start
  0.0 1.0 fusion
  1.0 0.2 fusion.1
  1.3 0.1 fusion.13
  1.4 0.9 select_reduce_fusion
  2.3 0.8 fusion.8.slot_ref
  3.1 0.1 convert_bitcast_fusion
  3.2 0.2 copy.30
  3.4 0.1 slice.8
  3.5 0.1 pad.8.starts_ref
  3.6 0.8 fusion.4
  4.4 0.1 pad.13.clone
  4.5 2.3 %maximum_maximum_fusion.rows_ref = bf16[144,8192]{1,0:T(8,128)(2,1)S(1)} fusion(bf16[1,8192]{1,0:T(2,128)(2,1)S(1)} %broadcast_in_dim.58, bf16[1,8192]{1,0:T(2,128)(2,1)S(1)} %broadcast_in_dim.57, bf16[132,8192]{1,0:T(8,128)(2,1)} %param.8, bf16[144]{0:T(256)(128)(2,1)S(1)} %pad.13.clone), kind=kLoop, calls=%fused_computation | loop fusion | flops 9437184 | bytes 4555040 | tf_op jit(solution)/shard_map/concatenate | solution.py:340
  6.8 25.9 %pack_rows.1.packed = bf16[8,144,2048]{2,1,0:T(8,128)(2,1)} custom-call(s32[8,17]{1,0:T(8,128)S(1)} %pad.8.starts_ref, bf16[144,8192]{1,0:T(8,128)(2,1)S(1)} %maximum_maximum_fusion.rows_ref, s32[1,8192]{1,0:T(1,128)S(1)} %fusion.8.slot_ref), custom_call_target="tpu_custom_call" | custom-call | tf_op jit(solution)/shard_map/pack_rows/pallas_call | solution.py:350
  32.7 0.0 copy-start.2
  32.7 0.0 copy-start.3
  32.7 0.0 copy-start.1
  32.7 0.0 copy-done
  32.8 0.2 copy.20
  33.0 1.1 add_divide_fusion
  34.1 0.0 copy-done.2
  34.1 0.0 copy-done.3
  34.1 0.7 select_bitcast_fusion
  34.8 0.0 copy-done.1
  34.8 2.6 %copy.17 = bf16[8,4,132,256]{3,2,1,0:T(8,128)(2,1)} copy(bf16[8,4,132,256]{3,1,0,2:T(4,128)(2,1)S(1)} %bitcast.31) | data formatting | bytes 4325376 | tf_op jit(solution)/shard_map/transpose | solution.py:360
  37.5 164.9 %exchange_advect_settle.1 = bf16[32,132,256]{2,1,0:T(8,128)(2,1)} custom-call(bf16[8,144,2048]{2,1,0:T(8,128)(2,1)} %pack_rows.1.packed, bf16[32,132,256]{2,1,0:T(8,128)(2,1)} %bitcast.30, f32[4,8,256]{2,1,0:T(8,128)} %get-tuple-element.10.cx, f32[4,8,256]{2,1,0:T(8,128)} %get-tuple-element.9.cy, f32[8,144,1]{2,1,0:T(8,128)} %get-tuple-element.6.scale, ...), custom_call_target="tpu_custom_call" | custom-call | tf_op jit(solution)/shard_map/exchange_advect_settle/pallas_call | solution.py:372
  202.3 4.2 %copy.29 = bf16[8,4,132,256]{3,1,0,2:T(4,128)(2,1)} copy(bf16[8,4,132,256]{3,2,1,0:T(8,128)(2,1)} %bitcast.29) | data formatting | bytes 4325376 | tf_op jit(solution)/shard_map/reshape | solution.py:399
  (7 shorter events, 0.1 us)
Async XLA Ops:
  0.0 32.7 %copy-start = (f32[132,32]{0,1:T(8,128)S(1)}, f32[132,32]{0,1:T(8,128)}, u32[]{:S(2)}) copy-start(f32[132,32]{0,1:T(8,128)} %param.13) | copy-start | bytes 50692
  32.7 1.4 copy-start.2
  32.7 1.4 copy-start.3
  32.7 2.1 %copy-start.1 = (bf16[132,8,4,256]{3,2,1,0:T(4,128)(2,1)S(1)}, bf16[132,8,4,256]{3,2,1,0:T(4,128)(2,1)}, u32[]{:S(2)}) copy-start(bf16[132,8,4,256]{3,2,1,0:T(4,128)(2,1)} %param.7) | copy-start | bytes 6488068

commit v4 on v3

--- a/solution.py
+++ b/solution.py
@@ -135,7 +135,7 @@
 
     lax.fori_loop(1, peers, start_rows, 0)
 
-    depth = min(1024, capacity)
+    depth = min(2048, capacity)
     bundle = 8
     lane_cells = lax.broadcasted_iota(jnp.int32, (width, depth), 0).astype(jnp.float32)
 

time: 207 us -> 204 us (0.986)
  Pallas kernels: 191 us -> 188 us
    pallas_call x1, Pallas kernels: 165 us -> 162 us  [per_device(): pl.pallas_call(functools.partial(main_kernel, comps), out_shape=jax.Shape...]
where the time goes in v4:
time: 204 us
  Pallas kernels  188 us (92%)
  local copies, waits for them, and re-layouts  7.79 us (4%)
  other arithmetic  6.72 us (3%)
    pallas_call x1, Pallas kernels, per_device(): pl.pallas_call(functools.partial(main_kernel, comps), out_shape=jax.Shape...  162 us
    pallas_call x1, Pallas kernels, per_device(): pl.pallas_call(functools.partial(pack_kernel, block), out_shape=jax.Shape...  26.2 us
    reshape x1, local copies, waits for them, and re-layouts, per_device(): settled = settled.reshape(levels, xcells, comps, ycells)  4.21 us

profile of v4, /device:TPU:24, one launch (start us, length us, event | category | flops | bytes accessed | tf_op | source)
XLA Modules:
  0.0 204.1 jit_solution(13710005429472453640)
XLA Ops:
  0.0 0.0 copy-start
  0.0 1.0 fusion
  1.0 0.2 fusion.1
  1.3 0.1 fusion.13
  1.4 0.9 select_reduce_fusion
  2.3 0.8 fusion.8.slot_ref
  3.1 0.1 convert_bitcast_fusion
  3.2 0.2 copy.30
  3.4 0.1 slice.8
  3.5 0.1 pad.8.starts_ref
  3.6 0.8 fusion.4
  4.4 0.1 pad.13.clone
  4.5 2.3 %maximum_maximum_fusion.rows_ref = bf16[144,8192]{1,0:T(8,128)(2,1)S(1)} fusion(bf16[1,8192]{1,0:T(2,128)(2,1)S(1)} %broadcast_in_dim.58, bf16[1,8192]{1,0:T(2,128)(2,1)S(1)} %broadcast_in_dim.57, bf16[132,8192]{1,0:T(8,128)(2,1)} %param.8, bf16[144]{0:T(256)(128)(2,1)S(1)} %pad.13.clone), kind=kLoop, calls=%fused_computation | loop fusion | flops 9437184 | bytes 4555040 | tf_op jit(solution)/shard_map/concatenate | solution.py:340
  6.8 26.2 %pack_rows.1.packed = bf16[8,144,2048]{2,1,0:T(8,128)(2,1)} custom-call(s32[8,17]{1,0:T(8,128)S(1)} %pad.8.starts_ref, bf16[144,8192]{1,0:T(8,128)(2,1)S(1)} %maximum_maximum_fusion.rows_ref, s32[1,8192]{1,0:T(1,128)S(1)} %fusion.8.slot_ref), custom_call_target="tpu_custom_call" | custom-call | tf_op jit(solution)/shard_map/pack_rows/pallas_call | solution.py:350
  33.0 0.0 copy-start.2
  33.0 0.0 copy-start.3
  33.0 0.0 copy-start.1
  33.0 0.0 copy-done
  33.0 0.2 copy.20
  33.2 1.1 add_divide_fusion
  34.3 0.0 copy-done.2
  34.4 0.0 copy-done.3
  34.4 0.7 select_bitcast_fusion
  35.1 0.0 copy-done.1
  35.1 2.6 %copy.17 = bf16[8,4,132,256]{3,2,1,0:T(8,128)(2,1)} copy(bf16[8,4,132,256]{3,1,0,2:T(4,128)(2,1)S(1)} %bitcast.31) | data formatting | bytes 4325376 | tf_op jit(solution)/shard_map/transpose | solution.py:360
  37.7 162.2 %exchange_advect_settle.1 = bf16[32,132,256]{2,1,0:T(8,128)(2,1)} custom-call(bf16[8,144,2048]{2,1,0:T(8,128)(2,1)} %pack_rows.1.packed, bf16[32,132,256]{2,1,0:T(8,128)(2,1)} %bitcast.30, f32[4,8,256]{2,1,0:T(8,128)} %get-tuple-element.10.cx, f32[4,8,256]{2,1,0:T(8,128)} %get-tuple-element.9.cy, f32[8,144,1]{2,1,0:T(8,128)} %get-tuple-element.6.scale, ...), custom_call_target="tpu_custom_call" | custom-call | tf_op jit(solution)/shard_map/exchange_advect_settle/pallas_call | solution.py:372
  199.9 4.2 %copy.29 = bf16[8,4,132,256]{3,1,0,2:T(4,128)(2,1)} copy(bf16[8,4,132,256]{3,2,1,0:T(8,128)(2,1)} %bitcast.29) | data formatting | bytes 4325376 | tf_op jit(solution)/shard_map/reshape | solution.py:399
  (7 shorter events, 0.1 us)
Async XLA Ops:
  0.0 33.0 %copy-start = (f32[132,32]{0,1:T(8,128)S(1)}, f32[132,32]{0,1:T(8,128)}, u32[]{:S(2)}) copy-start(f32[132,32]{0,1:T(8,128)} %param.13) | copy-start | bytes 50692
  33.0 1.4 copy-start.2
  33.0 1.4 copy-start.3
  33.0 2.1 %copy-start.1 = (bf16[132,8,4,256]{3,2,1,0:T(4,128)(2,1)S(1)}, bf16[132,8,4,256]{3,2,1,0:T(4,128)(2,1)}, u32[]{:S(2)}) copy-start(bf16[132,8,4,256]{3,2,1,0:T(4,128)(2,1)} %param.7) | copy-start | bytes 6488068

commit v5 on v4

--- a/solution.py
+++ b/solution.py
@@ -328,7 +328,7 @@
     capacity = 2 * row_count // peers
     height = up(comps + 2, 16)
     groups = levels * xcells
-    block = 512
+    block = 256
 
     targets = dest_tile[:, 0]
     member = (targets[None, :] == jnp.arange(peers, dtype=jnp.int32)[:, None]).astype(jnp.int32)

time: 204 us -> 210 us (1.029)
  Pallas kernels: 188 us -> 194 us
    pallas_call x1, Pallas kernels: 26.2 us -> 31.8 us  [per_device(): pl.pallas_call(functools.partial(pack_kernel, block), out_shape=jax.Shape...]
where the time goes in v5:
time: 210 us
  Pallas kernels  194 us (92%)
  local copies, waits for them, and re-layouts  7.81 us (4%)
  other arithmetic  6.73 us (3%)
    pallas_call x1, Pallas kernels, per_device(): pl.pallas_call(functools.partial(main_kernel, comps), out_shape=jax.Shape...  162 us
    pallas_call x1, Pallas kernels, per_device(): pl.pallas_call(functools.partial(pack_kernel, block), out_shape=jax.Shape...  31.8 us
    reshape x1, local copies, waits for them, and re-layouts, per_device(): settled = settled.reshape(levels, xcells, comps, ycells)  4.21 us

profile of v5, /device:TPU:24, one launch (start us, length us, event | category | flops | bytes accessed | tf_op | source)
XLA Modules:
  0.0 209.6 jit_solution(12528385874248694189)
XLA Ops:
  0.0 0.0 copy-start
  0.0 1.0 fusion
  1.0 0.2 fusion.1
  1.3 0.1 fusion.13
  1.4 0.9 select_reduce_fusion
  2.3 0.8 fusion.8.slot_ref
  3.1 0.1 convert_bitcast_fusion
  3.2 0.2 copy.30
  3.4 0.1 slice.8
  3.5 0.1 pad.8.starts_ref
  3.6 0.8 fusion.4
  4.5 0.1 pad.13.clone
  4.5 2.3 %maximum_maximum_fusion.rows_ref = bf16[144,8192]{1,0:T(8,128)(2,1)S(1)} fusion(bf16[1,8192]{1,0:T(2,128)(2,1)S(1)} %broadcast_in_dim.58, bf16[1,8192]{1,0:T(2,128)(2,1)S(1)} %broadcast_in_dim.57, bf16[132,8192]{1,0:T(8,128)(2,1)} %param.8, bf16[144]{0:T(256)(128)(2,1)S(1)} %pad.13.clone), kind=kLoop, calls=%fused_computation | loop fusion | flops 9437184 | bytes 4555040 | tf_op jit(solution)/shard_map/concatenate | solution.py:340
  6.8 31.8 %pack_rows.1.packed = bf16[8,144,2048]{2,1,0:T(8,128)(2,1)} custom-call(s32[8,33]{1,0:T(8,128)S(1)} %pad.8.starts_ref, bf16[144,8192]{1,0:T(8,128)(2,1)S(1)} %maximum_maximum_fusion.rows_ref, s32[1,8192]{1,0:T(1,128)S(1)} %fusion.8.slot_ref), custom_call_target="tpu_custom_call" | custom-call | tf_op jit(solution)/shard_map/pack_rows/pallas_call | solution.py:350
  38.6 0.0 copy-start.2
  38.6 0.0 copy-start.3
  38.6 0.0 copy-start.1
  38.6 0.0 copy-done
  38.6 0.2 copy.20
  38.9 1.1 add_divide_fusion
  40.0 0.0 copy-done.2
  40.0 0.0 copy-done.3
  40.0 0.7 select_bitcast_fusion
  40.7 0.0 copy-done.1
  40.7 2.6 %copy.17 = bf16[8,4,132,256]{3,2,1,0:T(8,128)(2,1)} copy(bf16[8,4,132,256]{3,1,0,2:T(4,128)(2,1)S(1)} %bitcast.31) | data formatting | bytes 4325376 | tf_op jit(solution)/shard_map/transpose | solution.py:360
  43.3 162.0 %exchange_advect_settle.1 = bf16[32,132,256]{2,1,0:T(8,128)(2,1)} custom-call(bf16[8,144,2048]{2,1,0:T(8,128)(2,1)} %pack_rows.1.packed, bf16[32,132,256]{2,1,0:T(8,128)(2,1)} %bitcast.30, f32[4,8,256]{2,1,0:T(8,128)} %get-tuple-element.10.cx, f32[4,8,256]{2,1,0:T(8,128)} %get-tuple-element.9.cy, f32[8,144,1]{2,1,0:T(8,128)} %get-tuple-element.6.scale, ...), custom_call_target="tpu_custom_call" | custom-call | tf_op jit(solution)/shard_map/exchange_advect_settle/pallas_call | solution.py:372
  205.4 4.2 %copy.29 = bf16[8,4,132,256]{3,1,0,2:T(4,128)(2,1)} copy(bf16[8,4,132,256]{3,2,1,0:T(8,128)(2,1)} %bitcast.29) | data formatting | bytes 4325376 | tf_op jit(solution)/shard_map/reshape | solution.py:399
  (7 shorter events, 0.1 us)
Async XLA Ops:
  0.0 38.6 %copy-start = (f32[132,32]{0,1:T(8,128)S(1)}, f32[132,32]{0,1:T(8,128)}, u32[]{:S(2)}) copy-start(f32[132,32]{0,1:T(8,128)} %param.13) | copy-start | bytes 50692
  38.6 1.4 copy-start.2
  38.6 1.4 copy-start.3
  38.6 2.1 %copy-start.1 = (bf16[132,8,4,256]{3,2,1,0:T(4,128)(2,1)S(1)}, bf16[132,8,4,256]{3,2,1,0:T(4,128)(2,1)}, u32[]{:S(2)}) copy-start(bf16[132,8,4,256]{3,2,1,0:T(4,128)(2,1)} %param.7) | copy-start | bytes 6488068
